TPU v7x, 512 devices: a whole 4x8x8 slice. The times are simulated.
512 devices in a mesh: dom: 128 (over y, z, core), grp: 4 (over x).
Axes of the slice: x: 4, y: 8, z: 8, core: 2. Of those that a mesh axis runs over, the one named last changes fastest.
Arguments:
- node_latent: bfloat16 [65536, 512], P(('dom', 'grp')), may hold values from -6 to 6
- edge_latent: bfloat16 [262144, 512], P(('dom', 'grp')), may hold values from -6 to 6
- coarse_edge_latent: bfloat16 [16384, 512], P('dom'), may hold values from -6 to 6
- w_source: bfloat16 [512, 512], replicated, may hold values from -0.25 to 0.25
- w_target: bfloat16 [512, 512], replicated, may hold values from -0.25 to 0.25
- w_node: bfloat16 [512, 512], replicated, may hold values from -0.25 to 0.25
- cotangent: bfloat16 [65536, 512], P(('dom', 'grp')), may hold values from -6 to 6
- halo_rows: int32 [512, 2, 32], P(('dom', 'grp')), may hold values from -1 to 127, as said below
- fine_src: int32 [262144], P(('dom', 'grp')), may hold values from -1 to 191, as said below
- fine_dst: int32 [262144], P(('dom', 'grp')), may hold values from -1 to 127, as said below
- coarse_src: int32 [16384], P('dom'), may hold values from -1 to 31, as said below
- coarse_dst: int32 [16384], P('dom'), may hold values from -1 to 31, as said below
- intersection_ids: int32 [2, 65536], P(None, ('dom', 'grp')), may hold values from 0 to 31, as said below
- intersection_weights: float32 [2, 65536], P(None, ('dom', 'grp')), may hold values from 0.05 to 0.5
Outputs:
- updated: bfloat16 [65536, 512], P(('dom', 'grp'))
- grad_latent: bfloat16 [65536, 512], P(('dom', 'grp'))
- grad_source: float32 [262144], P(('dom', 'grp'))
- grad_target: float32 [262144], P(('dom', 'grp'))
- grad_node: float32 [262144], P(('dom', 'grp'))
Inputs may be any that keep to these rules, and one draw needn't show every extreme that they name: `halo_rows`: in each list the first entries are rows of the subdomain, the rest -1; subdomain 0 sends nothing to side 0 and the last subdomain nothing to side 1. Per subdomain, the used edge slots come first and the others are -1, in fine_src and fine_dst alike; between 256 and 512 are used, some subdomain uses all. A source below 128 is a local row, 128 + j the j-th filled side-1 entry of the subdomain below, 160 + j the j-th filled side-0 entry of the subdomain above. `fine_dst`: -1 exactly where fine_src is -1. `coarse_src`: per group, the used slots come first, the others are -1 in both coarse lists; between 64 and 128 are used. `coarse_dst`: -1 exactly where coarse_src is -1. `intersection_ids`: coarse nodes of the fine node's own group; coarse node c is owned by the group's member c // 8.
All inputs are finite; a program needn't handle non-finite values.
Results may differ from a plain program's by a relative error of at most 0.017.
Values may be sent and summed in bfloat16 or wider, within the bound.
A program may use at most 64 MiB of HBM per device.

v0:
```python
from types import SimpleNamespace

import jax
import jax.numpy as jnp
from jax import lax
from jax.experimental import pallas as pl
from jax.experimental.pallas import tpu as pltpu
from jax.sharding import PartitionSpec as P

COARSE_DEV = 8
CORES = 2
EPSILON = 1e-06
VMEM_BYTES = 48 * 1024 * 1024
MESH = pl.DeviceIdType.MESH
BF16, F32, I32 = jnp.bfloat16, jnp.float32, jnp.int32


def nn(a, b):
    return lax.dot_general(a, b, (((1,), (0,)), ((), ())), preferred_element_type=F32)


def nt(a, b):
    return lax.dot_general(a, b, (((1,), (1,)), ((), ())), preferred_element_type=F32)


def tn(a, b):
    return lax.dot_general(a, b, (((0,), (0,)), ((), ())), preferred_element_type=F32)


def iota(shape, dim):
    return lax.broadcasted_iota(I32, shape, dim)


def hot(condition):
    return jnp.where(condition, 1.0, 0.0).astype(BF16)


def one_hot(positions, extent):
    return hot(iota((extent, positions.shape[1]), 0) == positions)


def restriction(ids, weights, extent):
    column = iota((extent, ids.shape[1]), 0)
    first = jnp.where(ids[0:1] == column, weights[0:1], 0.0)
    return first + jnp.where(ids[1:2] == column, weights[1:2], 0.0)


def silu_slope(preact):
    logistic = jax.nn.sigmoid(preact)
    return logistic * (1.0 + preact * (1.0 - logistic))


def mean_last(values):
    return jnp.mean(values, axis=-1, keepdims=True)


def fold(values):
    half = values.shape[1] // 2
    return jnp.concatenate([values[:, :half], values[:, half:]], axis=0)


def unfold(values):
    half = values.shape[0] // 2
    return jnp.concatenate([values[:half], values[half:]], axis=1)


def make_kernel(ny, nz, nx, width, nodes, edges, sends, coarse, cedges):
    half = width // CORES
    sizes = {"y": ny, "z": nz, "x": nx}
    plans = ((("z",), ("x", "y")), (("y",), ("x", "z")), (("x",), ("z",), ("y",)))

    def offsets(axes):
        places = [{}]
        for axis in axes:
            places = [{**place, axis: k} for place in places for k in range(sizes[axis])]
        return places

    def farthest_first(axes):
        places = offsets(axes)

        def hops(slot):
            return sum(min(k, sizes[axis] - k) for axis, k in places[slot].items())

        return sorted(range(1, len(places)), key=hops, reverse=True)
    table = nodes + nodes + 2 * sends
    reach, hops = 2, [1]
    while reach < max(ny, nz) // 2:
        hops.append(2)
        reach += 2
    hops.append(1)

    def vmem(*shape, kind=BF16):
        return pltpu.VMEM(shape, kind)

    def sems(*count):
        return pltpu.SemaphoreType.DMA(count)

    loaded = dict(
        node=vmem(nodes, width),
        edge=vmem(edges, width),
        cedge=vmem(cedges, width),
        ws=vmem(width, width),
        wt=vmem(width, width),
        wn=vmem(width, width),
        cot=vmem(nodes, width),
        halo=vmem(1, 2, sends, kind=I32),
        src=vmem(1, edges, kind=I32),
        dst=vmem(1, edges, kind=I32),
        csrc=vmem(1, cedges, kind=I32),
        cdst=vmem(1, cedges, kind=I32),
        ids=vmem(2, nodes, kind=I32),
        wts=vmem(2, nodes, kind=F32),
    )
    work = dict(
        oht=vmem(table, edges),
        oh=vmem(edges, table),
        proj=vmem(table, width),
        pre=vmem(edges, width, kind=F32),
        msg=vmem(edges, width),
        normed=vmem(nodes, width, kind=F32),
        fine_out=vmem(nodes, width, kind=F32),
        in_sem=sems(len(loaded)),
        hello=pltpu.SemaphoreType.REGULAR((len(hops),)),
    )

    def exchange(out, into, count):
        return dict(out=out, into=into, ss=sems(count), rs=sems(count))

    rows = vmem(2 * sends, width)
    halves = [exchange(rows, rows, 2) for _ in range(2)]
    sums = [exchange(vmem(coarse, width), vmem(nx - 1, coarse, width), nx - 1) for _ in range(2)]
    streams = []
    for i, plan in enumerate(plans):
        first = vmem(half, width)
        levels = [exchange(first, first, 1)]
        size = half
        for axes in plan:
            count = len(offsets(axes))
            size = size // count
            if axes is plan[-1]:
                buffer = vmem(count - 1, size, width, kind=F32)
            elif axes is plan[0]:
                buffer = vmem(count - 1, size, width)
            else:
                buffer = vmem(count - 1, 2 * size, width // 2)
            levels.append(exchange(buffer, buffer, count - 1))
        streams.append(
            dict(
                perm=vmem(width, width),
                left=vmem(width, nodes + coarse + (2 * sends if i == 0 else 0)),
                keep=vmem(half, width, kind=F32),
                levels=levels,
            )
        )
    scratch = [loaded, work, halves, sums, streams]

    def kernel(*refs):
        count = len(loaded)
        given, outs = refs[:count], refs[count : count + 5]
        held, work, halves, sums, streams = refs[count + 5 :]
        v = SimpleNamespace(**held, **work)
        halves, sums = ([SimpleNamespace(**e) for e in group] for group in (halves, sums))
        streams = [SimpleNamespace(**stream) for stream in streams]
        for stream in streams:
            stream.levels = [SimpleNamespace(**level) for level in stream.levels]
        for stream, plan, row in zip(streams, plans, outs[2:]):
            stream.plan, stream.row = plan, row
        source_stream, target_stream, node_stream = streams
        halo_rows, back_rows = halves
        cot_sum, val_sum = sums
        dom, x = lax.axis_index("dom"), lax.axis_index("grp")
        core = lax.rem(dom, CORES)
        z = lax.rem(lax.div(dom, CORES), nz)
        y = lax.div(dom, CORES * nz)
        ring = dict(
            x=[x] + [lax.rem(x + k, nx) for k in range(1, nx)],
            y=[y] + [lax.rem(y + k, ny) for k in range(1, ny)],
            z=[z] + [lax.rem(z + k, nz) for k in range(1, nz)],
        )

        loads = SimpleNamespace(
            **{
                name: pltpu.make_async_copy(ref, held[name], v.in_sem.at[i])
                for i, (name, ref) in enumerate(zip(loaded, given))
            }
        )

        def place(y, z, core, x):
            return ((y * nz + z) * CORES + core, x)

        def at(shift):
            return place(
                ring["y"][shift.get("y", 0)],
                ring["z"][shift.get("z", 0)],
                core,
                ring["x"][shift.get("x", 0)],
            )

        twin = place(y, z, 1 - core, x)
        total = ny * nz * CORES * nx
        here = dom * nx + x
        above, below = lax.rem(here + 1, total), lax.rem(here + total - 1, total)
        above, below = ((lax.div(n, nx), lax.rem(n, nx)) for n in (above, below))

        barrier = pltpu.get_barrier_semaphore()
        around = [at({"y": 1}), at({"y": ny - 1}), at({"z": 1}), at({"z": nz - 1})]
        partners = [above, below] + [at({"x": k}) for k in range(1, nx)] + around + [twin]
        for partner in partners:
            pl.semaphore_signal(barrier, inc=1, device_id=partner, device_id_type=MESH)

        for load in (
            loads.halo,
            loads.node,
            loads.src,
            loads.dst,
            loads.ids,
            loads.wts,
            loads.csrc,
            loads.cdst,
            loads.cot,
            loads.wt,
            loads.ws,
            loads.edge,
            loads.wn,
            loads.cedge,
        ):
            load.start()

        def tell(step):
            hop = hops[step]
            for shift in ({"y": hop}, {"y": ny - hop}, {"z": hop}, {"z": nz - hop}):
                pl.semaphore_signal(
                    v.hello.at[step], inc=1, device_id=at(shift), device_id_type=MESH
                )

        def hear(step):
            pl.semaphore_wait(v.hello.at[step], len(around))

        def remote(source, target, send_sem, recv_sem, device):
            return pltpu.make_async_remote_copy(
                src_ref=source,
                dst_ref=target,
                send_sem=send_sem,
                recv_sem=recv_sem,
                device_id=device,
                device_id_type=MESH,
            )

        started = []

        def settle():
            for copy in started:
                copy.wait_send()
            started.clear()

        def start(copies):
            for copy in copies:
                copy.start()
            started.extend(copies)
            return copies

        loads.halo.wait()
        lists = v.halo[0]
        side = [one_hot(lists[s : s + 1], nodes) for s in range(2)]
        loads.node.wait()
        node = v.node[...]
        for s in range(2):
            halo_rows.out[s * sends : (s + 1) * sends] = tn(side[s], node).astype(BF16)
        low, high = pl.ds(0, sends), pl.ds(sends, sends)
        pl.semaphore_wait(barrier, len(partners))

        def to_neighbours(e):
            return start(
                [
                    remote(e.out.at[low], e.into.at[high], e.ss.at[0], e.rs.at[0], below),
                    remote(e.out.at[high], e.into.at[low], e.ss.at[1], e.rs.at[1], above),
                ]
            )

        def to_peer(e, source, axes, slot):
            copy = remote(
                source, e.into.at[slot - 1], e.ss.at[slot - 1], e.rs.at[slot - 1], at(offsets(axes)[slot])
            )
            return start([copy])[0]

        def to_group(e):
            return [to_peer(e, e.out, ("x",), slot) for slot in farthest_first(("x",))]

        def group_sum(e, copies):
            for copy in copies:
                copy.wait_recv()
            running = e.out[...].astype(F32)
            for k in range(nx - 1):
                running = running + e.into[k].astype(F32)
            return running

        halo = to_neighbours(halo_rows)
        tell(0)
        loads.ids.wait()
        loads.wts.wait()
        restrict = restriction(v.ids[...], v.wts[...], coarse).astype(BF16)
        loads.cot.wait()
        cot_sum.out[...] = nn(restrict, v.cot[...]).astype(BF16)
        cot_copies = to_group(cot_sum)

        loads.src.wait()
        loads.dst.wait()
        v.oht[0:nodes] = one_hot(v.dst[...], nodes)
        v.oht[nodes:] = one_hot(v.src[...], table - nodes)
        eye = hot(iota((edges, edges), 0) == iota((edges, edges), 1))
        v.oh[...] = nt(eye, v.oht[...]).astype(BF16)
        loads.wt.wait()
        v.proj[0:nodes] = nn(node, v.wt[...]).astype(BF16)
        loads.ws.wait()
        v.proj[nodes : 2 * nodes] = nn(node, v.ws[...]).astype(BF16)
        loads.edge.wait()
        chunk = edges // 4
        local = 2 * nodes
        for e in range(0, edges, chunk):
            rows = slice(e, e + chunk)
            v.pre[rows] = v.edge[rows].astype(F32) + nn(
                v.oh[rows, 0:local], v.proj[0:local]
            )
        for copy in halo:
            copy.wait_recv()
        hear(0)
        tell(1)
        v.proj[local:] = nn(halo_rows.into[...], v.ws[...]).astype(BF16)
        for e in range(0, edges, chunk):
            rows = slice(e, e + chunk)
            preact = v.pre[rows] + nn(v.oh[rows, local:], v.proj[local:])
            v.pre[rows] = preact
            v.msg[rows] = jax.nn.silu(preact).astype(BF16)
        summed = nn(v.oht[0:nodes], v.msg[...])
        inverse = lax.rsqrt(mean_last(summed * summed) + EPSILON)
        normed = summed * inverse
        v.normed[...] = normed
        normed_half = normed.astype(BF16)
        loads.wn.wait()
        fine_out = node.astype(F32) + nn(normed_half, v.wn[...])
        v.fine_out[...] = fine_out
        val_sum.out[...] = nn(restrict, fine_out.astype(BF16)).astype(BF16)
        val_copies = to_group(val_sum)

        for stream in streams:
            order = [axis for axes in stream.plan for axis in axes]
            rest = iota((width, width), 0)
            digits = {}
            for axis in reversed(order):
                digits[axis] = rest % sizes[axis]
                rest = rest // sizes[axis]
            owner_core = jnp.where(rest == 0, 1 - core, core)
            row = ((y + digits["y"]) % ny) * nz + (z + digits["z"]) % nz
            row = (row * CORES + owner_core) * nx + (x + digits["x"]) % nx
            stream.perm[...] = hot(row == iota((width, width), 1))
        source_stream.left[:, 0:nodes] = nt(source_stream.perm[...], node).astype(BF16)
        source_stream.left[:, nodes : nodes + 2 * sends] = nt(
            source_stream.perm[...], halo_rows.into[...]
        ).astype(BF16)
        target_stream.left[:, 0:nodes] = nt(target_stream.perm[...], node).astype(BF16)
        node_stream.left[:, 0:nodes] = nt(node_stream.perm[...], normed_half).astype(BF16)
        for stream in streams:
            stream.left[:, -coarse:] = jnp.zeros((width, coarse), BF16)
        for e in range(0, edges, chunk):
            rows = slice(e, e + chunk)
            v.pre[rows] = silu_slope(v.pre[rows])
        loads.csrc.wait()
        loads.cdst.wait()
        coarse_hot_t = jnp.concatenate(
            [one_hot(v.cdst[...], coarse), one_hot(v.csrc[...], coarse)], axis=0
        )
        eye = hot(iota((cedges, cedges), 0) == iota((cedges, cedges), 1))
        coarse_hot = nt(eye, coarse_hot_t).astype(BF16)
        eye = hot(iota((nodes, nodes), 0) == iota((nodes, nodes), 1))
        prolong = nt(eye, restrict).astype(BF16)
        grad_coarse = group_sum(cot_sum, cot_copies)
        grad_coarse_half = grad_coarse.astype(BF16)
        coarse_normed_grad = nt(grad_coarse_half, v.wn[...])
        loads.cedge.wait()
        coarse_edge = v.cedge[...].astype(F32)

        for step in range(1, len(hops) - 1):
            hear(step)
            tell(step + 1)
        coarse_half = group_sum(val_sum, val_copies).astype(BF16)
        coarse_proj = jnp.concatenate(
            [nn(coarse_half, v.wt[...]), nn(coarse_half, v.ws[...])], axis=0
        ).astype(BF16)
        quarter = width // nx
        rows = pl.ds(pl.multiple_of(x * quarter, quarter), quarter)
        preact = coarse_edge + nn(coarse_hot, coarse_proj)
        target_stream.left[rows, nodes:] = nt(target_stream.perm[rows], coarse_half).astype(BF16)
        source_stream.left[rows, nodes + 2 * sends :] = nt(
            source_stream.perm[rows], coarse_half
        ).astype(BF16)
        message = jax.nn.silu(preact).astype(BF16)
        summed = nn(coarse_hot_t[0:coarse], message)
        coarse_inverse = lax.rsqrt(mean_last(summed * summed) + EPSILON)
        coarse_normed = summed * coarse_inverse
        coarse_normed_half = coarse_normed.astype(BF16)
        for begin in range(0, width, half):
            rows = slice(begin, begin + half // nx)
            node_stream.left[rows, nodes:] = nt(node_stream.perm[rows], coarse_normed_half).astype(
                BF16
            )
        grad_summed = coarse_inverse * (
            coarse_normed_grad - coarse_normed * mean_last(coarse_normed_grad * coarse_normed)
        )
        grad_preact = (
            nn(coarse_hot[:, 0:coarse], grad_summed.astype(BF16)) * silu_slope(preact)
        ).astype(BF16)
        coarse_grad = nn(coarse_hot_t, grad_preact).astype(BF16)
        grad_coarse_in = (
            grad_coarse
            + nt(coarse_grad[coarse:], v.ws[...])
            + nt(coarse_grad[0:coarse], v.wt[...])
        )
        grad_fine = v.cot[...].astype(F32) + nn(prolong, grad_coarse_in.astype(BF16))
        grad_half = grad_fine.astype(BF16)

        def stage0(stream, right):
            e = stream.levels[0]
            e.out[...] = nn(stream.left[0:half], right).astype(BF16)
            copies = start([remote(e.out, e.into, e.ss.at[0], e.rs.at[0], twin)])
            return copies

        def stage0_own(stream, right):
            stream.keep[...] = nn(stream.left[half:], right)

        def stage1(stream, copies):
            axes = stream.plan[0]
            size = half // len(offsets(axes))
            e, keep, into = stream.levels[1], stream.keep, stream.levels[0].into
            copies[0].wait_recv()
            sent = []
            for slot in farthest_first(axes):
                rows = slice(slot * size, (slot + 1) * size)
                e.out[slot - 1] = (keep[rows] + into[rows].astype(F32)).astype(BF16)
                sent.append(to_peer(e, e.out.at[slot - 1], axes, slot))
            keep[0:size] = keep[0:size] + into[0:size].astype(F32)
            return sent

        def received1(stream, copies):
            size = half // len(offsets(stream.plan[0]))
            running = stream.keep[0:size]
            for slot, copy in zip(reversed(farthest_first(stream.plan[0])), reversed(copies)):
                copy.wait_recv()
                running = running + stream.levels[1].into[slot - 1].astype(F32)
            return running

        def stage2(stream, copies):
            axes = stream.plan[1]
            running = received1(stream, copies)
            size = running.shape[0] // len(offsets(axes))
            e, sent = stream.levels[2], []
            for slot in farthest_first(axes):
                part = fold(running[slot * size : (slot + 1) * size])
                e.out[slot - 1] = part.astype(BF16)
                sent.append(to_peer(e, e.out.at[slot - 1], axes, slot))
            return sent, running[0:size]

        def received2(stream, state):
            copies, running = state
            for copy in reversed(copies):
                copy.wait_recv()
            for k in range(len(copies)):
                running = running + unfold(stream.levels[2].into[k].astype(F32))
            return running

        def last(stream, running, slots):
            e, axes, sent = stream.levels[-1], stream.plan[-1], []
            for slot in slots:
                e.out[slot - 1] = running[slot : slot + 1]
                sent.append(to_peer(e, e.out.at[slot - 1], axes, slot))
            return sent

        def halved(slots):
            middle = len(slots) // 2
            return slots[:middle], slots[middle:]

        def finish(stream, copies, running):
            for copy in reversed(copies):
                copy.wait_recv()
            stream.row[...] = running[0:1] + jnp.sum(stream.levels[-1].into[...], axis=0)

        right = jnp.concatenate([grad_half, grad_coarse_half], axis=0)
        node_state = stage0(node_stream, right)
        stage0_own(node_stream, right)

        grad_normed = nt(grad_half, v.wn[...])
        normed = v.normed[...]
        grad_summed = inverse * (grad_normed - normed * mean_last(grad_normed * normed))
        grad_summed = grad_summed.astype(BF16)
        for e in range(0, edges, chunk):
            rows = slice(e, e + chunk)
            v.msg[rows] = (nn(v.oh[rows, 0:nodes], grad_summed) * v.pre[rows]).astype(BF16)
        scattered = nn(v.oht[...], v.msg[...]).astype(BF16)
        grad_dst, grad_src = scattered[0:nodes], scattered[nodes:]
        target_right = jnp.concatenate([grad_dst, coarse_grad[0:coarse]], axis=0)
        target_state = stage0(target_stream, target_right)
        source_right = jnp.concatenate([grad_src, coarse_grad[coarse:]], axis=0)
        source_state = stage0(source_stream, source_right)
        node_state = stage1(node_stream, node_state)
        stage0_own(target_stream, target_right)
        stage0_own(source_stream, source_right)
        target_state = stage1(target_stream, target_state)
        source_state = stage1(source_stream, source_state)
        back_rows.out[...] = nt(grad_src[nodes:], v.ws[...]).astype(BF16)
        back = to_neighbours(back_rows)
        grad_latent = grad_fine + nt(grad_src[0:nodes], v.ws[...]) + nt(grad_dst, v.wt[...])
        coarse_out = coarse_half.astype(F32) + nn(coarse_normed_half, v.wn[...])
        updated = v.fine_out[...] + nn(prolong, coarse_out.astype(BF16))
        outs[0][...] = updated.astype(BF16)
        node_state = stage2(node_stream, node_state)
        for copy in back:
            copy.wait_recv()
        for s in range(2):
            grad_latent = grad_latent + nn(side[s], back_rows.into[s * sends : (s + 1) * sends])
        outs[1][...] = grad_latent.astype(BF16)
        target_far, target_near = halved(farthest_first(target_stream.plan[-1]))
        source_far, source_near = halved(farthest_first(source_stream.plan[-1]))
        hear(len(hops) - 1)
        target_sum = received1(target_stream, target_state)
        target_state = last(target_stream, target_sum, target_far)
        source_sum = received1(source_stream, source_state)
        source_state = last(source_stream, source_sum, source_far)
        node_sum = received2(node_stream, node_state)
        node_state = last(node_stream, node_sum, farthest_first(node_stream.plan[-1]))
        target_state += last(target_stream, target_sum, target_near)
        source_state += last(source_stream, source_sum, source_near)
        settle()
        finish(node_stream, node_state, node_sum)
        finish(target_stream, target_state, target_sum)
        finish(source_stream, source_state, source_sum)

    return kernel, scratch


def write_out(*refs):
    count = len(refs) // 2
    sems = refs[-1]
    copies = [pltpu.make_async_copy(refs[i], refs[count + i], sems.at[i]) for i in range(count)]
    for copy in copies:
        copy.start()
    for copy in copies:
        copy.wait()


def solution(mesh):
    nx = mesh.shape["grp"]
    chips = mesh.shape["dom"] // CORES
    ny = 1
    while ny * ny < chips:
        ny += 1
    nz = chips // ny

    def step(node, edge, cedge, ws, wt, wn, cot, halo, src, dst, csrc, cdst, ids, weights):
        nodes, width = node.shape
        kernel, scratch = make_kernel(
            ny,
            nz,
            nx,
            width,
            nodes,
            edge.shape[0],
            halo.shape[2],
            COARSE_DEV * nx,
            cedge.shape[0],
        )
        row = jax.ShapeDtypeStruct((1, width), F32)
        rows = jax.ShapeDtypeStruct((nodes, width), BF16)
        shapes = (rows, rows, row, row, row)
        lists = [given.reshape(1, -1) for given in (src, dst, csrc, cdst)]
        arguments = (node, edge, cedge, ws, wt, wn, cot, halo, *lists, ids, weights)
        held = pl.pallas_call(
            kernel,
            out_shape=tuple(pltpu.VMEM(shape.shape, shape.dtype) for shape in shapes),
            in_specs=[pl.BlockSpec(memory_space=pltpu.HBM)] * 14,
            out_specs=[pl.BlockSpec(memory_space=pltpu.VMEM)] * 5,
            scratch_shapes=scratch,
            compiler_params=pltpu.CompilerParams(
                collective_id=0, has_side_effects=True, vmem_limit_bytes=VMEM_BYTES
            ),
        )(*(pltpu.with_memory_space_constraint(given, pltpu.HBM) for given in arguments))
        updated, latent, gs, gt, gn = pl.pallas_call(
            write_out,
            out_shape=shapes,
            in_specs=[pl.BlockSpec(memory_space=pltpu.VMEM)] * 5,
            out_specs=[pl.BlockSpec(memory_space=pltpu.HBM)] * 5,
            scratch_shapes=[pltpu.SemaphoreType.DMA((5,))],
            compiler_params=pltpu.CompilerParams(vmem_limit_bytes=VMEM_BYTES),
        )(*held)
        return updated, latent, gs.reshape(-1), gt.reshape(-1), gn.reshape(-1)

    fine = P(("dom", "grp"), None)
    flat = P(("dom", "grp"))
    return jax.shard_map(
        step,
        mesh=mesh,
        in_specs=(
            fine,
            fine,
            P("dom", None),
            P(),
            P(),
            P(),
            fine,
            P(("dom", "grp"), None, None),
            flat,
            flat,
            P("dom"),
            P("dom"),
            P(None, ("dom", "grp")),
            P(None, ("dom", "grp")),
        ),
        out_specs=(fine, fine, flat, flat, flat),
        check_vma=False,
    )
```

profile of v0, /device:TPU:1, one launch (start us, length us, event | category | flops | bytes accessed | tf_op | source)
XLA Modules:
  0.0 45.1 jit_solution(4248026046058362058)
XLA Ops:
  0.6 43.7 %shard_map.173 = (bf16[128,512]{1,0:T(8,128)(2,1)S(1)}, bf16[128,512]{1,0:T(8,128)(2,1)S(1)}, f32[1,512]{1,0:T(1,128)S(1)}, f32[1,512]{1,0:T(1,128)S(1)}, f32[1,512]{1,0:T(1,128)S(1)}) custom-call(bf16[128,512]{1,0:T(8,128)(2,1)} %refs_0_.1, bf16[512,512]{1,0:T(8,128)(2,1)} %refs_1_.1, bf16[128,512]{1,0:T(8,128)(2,1)} %refs_2_.1, bf16[512,512]{1,0:T(8,128)(2,1)} %refs_3_.1, ...), custom_call_target="tpu_custom_call" | custom-call | tf_op jit(solution)/shard_map/pallas_call | solution.py:575
  44.4 0.8 %shard_map.174 = (bf16[128,512]{1,0:T(8,128)(2,1)}, bf16[128,512]{1,0:T(8,128)(2,1)}, f32[1,512]{1,0:T(1,128)}, f32[1,512]{1,0:T(1,128)}, f32[1,512]{1,0:T(1,128)}) custom-call(bf16[128,512]{1,0:T(8,128)(2,1)S(1)} %get-tuple-element.15.refs_0_, bf16[128,512]{1,0:T(8,128)(2,1)S(1)} %get-tuple-element.16.refs_1_, f32[1,512]{1,0:T(1,128)S(1)} %get-tuple-element.17.refs_2_, ...), custom_call_target="tpu_custom_call" | custom-call | tf_op jit(solution)/shard_map/pallas_call | solution.py:585
where the time goes:
time: 45.2 us; the launch traced here: 45.1 us
  Pallas kernels  44.5 us (98%)
  between operations  0.65 us (1%)
    pallas_call x1, Pallas kernels, step(): pl.pallas_call(kernel, out_shape=tuple((pltpu.VMEM(shape.shape, shape.dty...  43.7 us

commit v1 on v0

--- a/solution.py
+++ b/solution.py
@@ -131,8 +131,9 @@
     sums = [exchange(vmem(coarse, width), vmem(nx - 1, coarse, width), nx - 1) for _ in range(2)]
     streams = []
     for i, plan in enumerate(plans):
-        first = vmem(half, width)
-        levels = [exchange(first, first, 1)]
+        parts = 1
+        first = vmem(parts, half, width // parts)
+        levels = [exchange(first, first, parts)]
         size = half
         for axes in plan:
             count = len(offsets(axes))
@@ -140,10 +141,10 @@
             if axes is plan[-1]:
                 buffer = vmem(count - 1, size, width, kind=F32)
             elif axes is plan[0]:
-                buffer = vmem(count - 1, size, width)
+                buffer = vmem(parts * (count - 1), size, width // parts)
             else:
                 buffer = vmem(count - 1, 2 * size, width // 2)
-            levels.append(exchange(buffer, buffer, count - 1))
+            levels.append(exchange(buffer, buffer, buffer.shape[0]))
         streams.append(
             dict(
                 perm=vmem(width, width),
@@ -165,6 +166,9 @@
             stream.levels = [SimpleNamespace(**level) for level in stream.levels]
         for stream, plan, row in zip(streams, plans, outs[2:]):
             stream.plan, stream.row = plan, row
+            stream.parts = stream.levels[0].out.shape[0]
+            step = width // stream.parts
+            stream.columns = [slice(i * step, (i + 1) * step) for i in range(stream.parts)]
         source_stream, target_stream, node_stream = streams
         halo_rows, back_rows = halves
         cot_sum, val_sum = sums
@@ -277,9 +281,10 @@
                 ]
             )
 
-        def to_peer(e, source, axes, slot):
+        def to_peer(e, source, axes, slot, base=-1):
+            i = base + slot
             copy = remote(
-                source, e.into.at[slot - 1], e.ss.at[slot - 1], e.rs.at[slot - 1], at(offsets(axes)[slot])
+                source, e.into.at[i], e.ss.at[i], e.rs.at[i], at(offsets(axes)[slot])
             )
             return start([copy])[0]
 
@@ -418,39 +423,55 @@
         grad_fine = v.cot[...].astype(F32) + nn(prolong, grad_coarse_in.astype(BF16))
         grad_half = grad_fine.astype(BF16)
 
-        def stage0(stream, right):
+        def stage0(stream, right, part=0):
             e = stream.levels[0]
-            e.out[...] = nn(stream.left[0:half], right).astype(BF16)
-            copies = start([remote(e.out, e.into, e.ss.at[0], e.rs.at[0], twin)])
-            return copies
-
-        def stage0_own(stream, right):
-            stream.keep[...] = nn(stream.left[half:], right)
-
-        def stage1(stream, copies):
-            axes = stream.plan[0]
-            size = half // len(offsets(axes))
-            e, keep, into = stream.levels[1], stream.keep, stream.levels[0].into
-            copies[0].wait_recv()
-            sent = []
-            for slot in farthest_first(axes):
-                rows = slice(slot * size, (slot + 1) * size)
-                e.out[slot - 1] = (keep[rows] + into[rows].astype(F32)).astype(BF16)
-                sent.append(to_peer(e, e.out.at[slot - 1], axes, slot))
-            keep[0:size] = keep[0:size] + into[0:size].astype(F32)
+            e.out[part] = nn(stream.left[0:half], right).astype(BF16)
+            copy = remote(e.out.at[part], e.into.at[part], e.ss.at[part], e.rs.at[part], twin)
+            return start([copy])[0]
+
+        def stage0_own(stream, right, part=0):
+            stream.keep[:, stream.columns[part]] = nn(stream.left[half:], right)
+
+        def stage1(group, copies, part=0):
+            for copy in copies:
+                copy.wait_recv()
+            sent = [[] for _ in group]
+            for slots in zip(*(farthest_first(stream.plan[0]) for stream in group)):
+                for stream, slot, into in zip(group, slots, sent):
+                    e, axes = stream.levels[1], stream.plan[0]
+                    count = len(offsets(axes))
+                    size = half // count
+                    rows = slice(slot * size, (slot + 1) * size)
+                    i = part * (count - 1) + slot - 1
+                    e.out[i] = (
+                        stream.keep[rows, stream.columns[part]]
+                        + stream.levels[0].into[part, rows].astype(F32)
+                    ).astype(BF16)
+                    into.append(to_peer(e, e.out.at[i], axes, slot, part * (count - 1) - 1))
+            for stream in group:
+                rows = slice(0, half // len(offsets(stream.plan[0])))
+                columns = stream.columns[part]
+                stream.keep[rows, columns] = stream.keep[rows, columns] + stream.levels[0].into[
+                    part, rows
+                ].astype(F32)
             return sent
 
         def received1(stream, copies):
-            size = half // len(offsets(stream.plan[0]))
-            running = stream.keep[0:size]
-            for slot, copy in zip(reversed(farthest_first(stream.plan[0])), reversed(copies)):
-                copy.wait_recv()
-                running = running + stream.levels[1].into[slot - 1].astype(F32)
-            return running
+            slots = farthest_first(stream.plan[0])
+            size = half // (len(slots) + 1)
+            halves = []
+            for part, columns in enumerate(stream.columns):
+                running = stream.keep[0:size, columns]
+                for slot, copy in zip(reversed(slots), reversed(copies[part])):
+                    copy.wait_recv()
+                    i = part * len(slots) + slot - 1
+                    running = running + stream.levels[1].into[i].astype(F32)
+                halves.append(running)
+            return jnp.concatenate(halves, axis=1)
 
         def stage2(stream, copies):
             axes = stream.plan[1]
-            running = received1(stream, copies)
+            running = received1(stream, [copies])
             size = running.shape[0] // len(offsets(axes))
             e, sent = stream.levels[2], []
             for slot in farthest_first(axes):
@@ -485,26 +506,42 @@
 
         right = jnp.concatenate([grad_half, grad_coarse_half], axis=0)
         node_state = stage0(node_stream, right)
-        stage0_own(node_stream, right)
 
         grad_normed = nt(grad_half, v.wn[...])
         normed = v.normed[...]
         grad_summed = inverse * (grad_normed - normed * mean_last(grad_normed * normed))
         grad_summed = grad_summed.astype(BF16)
-        for e in range(0, edges, chunk):
-            rows = slice(e, e + chunk)
-            v.msg[rows] = (nn(v.oh[rows, 0:nodes], grad_summed) * v.pre[rows]).astype(BF16)
-        scattered = nn(v.oht[...], v.msg[...]).astype(BF16)
-        grad_dst, grad_src = scattered[0:nodes], scattered[nodes:]
-        target_right = jnp.concatenate([grad_dst, coarse_grad[0:coarse]], axis=0)
-        target_state = stage0(target_stream, target_right)
-        source_right = jnp.concatenate([grad_src, coarse_grad[coarse:]], axis=0)
-        source_state = stage0(source_stream, source_right)
-        node_state = stage1(node_stream, node_state)
-        stage0_own(target_stream, target_right)
-        stage0_own(source_stream, source_right)
-        target_state = stage1(target_stream, target_state)
-        source_state = stage1(source_stream, source_state)
+        edge_streams = (target_stream, source_stream)
+        rights, twins = [], []
+        for part, columns in enumerate(target_stream.columns):
+            for e in range(0, edges, chunk):
+                rows = slice(e, e + chunk)
+                part_grad = nn(v.oh[rows, 0:nodes], grad_summed[:, columns])
+                v.msg[rows, columns] = (part_grad * v.pre[rows, columns]).astype(BF16)
+            scattered = nn(v.oht[...], v.msg[:, columns]).astype(BF16)
+            rights.append(
+                [
+                    jnp.concatenate([scattered[0:nodes], coarse_grad[0:coarse, columns]], axis=0),
+                    jnp.concatenate([scattered[nodes:], coarse_grad[coarse:, columns]], axis=0),
+                ]
+            )
+            twins.append(
+                [stage0(stream, r, part) for stream, r in zip(edge_streams, rights[-1])]
+            )
+        stage0_own(node_stream, right)
+        node_state = stage1([node_stream], [node_state])[0]
+        target_state, source_state = [], []
+        for part in range(len(twins)):
+            for stream, r in zip(edge_streams, rights[part]):
+                stage0_own(stream, r, part)
+        for part in range(len(twins)):
+            to_target, to_source = stage1(edge_streams, twins[part], part)
+            target_state.append(to_target)
+            source_state.append(to_source)
+        grad_dst, grad_src = (
+            jnp.concatenate([part[i][:count] for part in rights], axis=1)
+            for i, count in ((0, nodes), (1, nodes + 2 * sends))
+        )
         back_rows.out[...] = nt(grad_src[nodes:], v.ws[...]).astype(BF16)
         back = to_neighbours(back_rows)
         grad_latent = grad_fine + nt(grad_src[0:nodes], v.ws[...]) + nt(grad_dst, v.wt[...])

time: 45.2 us -> 45.2 us (level)
  no operation moved by 1% of the time
where the time goes in v1:
time: 45.2 us; the launch traced here: 45.1 us
  Pallas kernels  44.5 us (98%)
  between operations  0.65 us (1%)
    pallas_call x1, Pallas kernels, step(): pl.pallas_call(kernel, out_shape=tuple((pltpu.VMEM(shape.shape, shape.dty...  43.7 us

profile of v1, /device:TPU:1, one launch (start us, length us, event | category | flops | bytes accessed | tf_op | source)
XLA Modules:
  0.0 45.1 jit_solution(9264403593062339272)
XLA Ops:
  0.6 43.7 %shard_map.173 = (bf16[128,512]{1,0:T(8,128)(2,1)S(1)}, bf16[128,512]{1,0:T(8,128)(2,1)S(1)}, f32[1,512]{1,0:T(1,128)S(1)}, f32[1,512]{1,0:T(1,128)S(1)}, f32[1,512]{1,0:T(1,128)S(1)}) custom-call(bf16[128,512]{1,0:T(8,128)(2,1)} %refs_0_.1, bf16[512,512]{1,0:T(8,128)(2,1)} %refs_1_.1, bf16[128,512]{1,0:T(8,128)(2,1)} %refs_2_.1, bf16[512,512]{1,0:T(8,128)(2,1)} %refs_3_.1, ...), custom_call_target="tpu_custom_call" | custom-call | tf_op jit(solution)/shard_map/pallas_call | solution.py:612
  44.4 0.8 %shard_map.174 = (bf16[128,512]{1,0:T(8,128)(2,1)}, bf16[128,512]{1,0:T(8,128)(2,1)}, f32[1,512]{1,0:T(1,128)}, f32[1,512]{1,0:T(1,128)}, f32[1,512]{1,0:T(1,128)}) custom-call(bf16[128,512]{1,0:T(8,128)(2,1)S(1)} %get-tuple-element.15.refs_0_, bf16[128,512]{1,0:T(8,128)(2,1)S(1)} %get-tuple-element.16.refs_1_, f32[1,512]{1,0:T(1,128)S(1)} %get-tuple-element.17.refs_2_, ...), custom_call_target="tpu_custom_call" | custom-call | tf_op jit(solution)/shard_map/pallas_call | solution.py:622
